TPU v7x, 256 devices: a whole 4x4x8 slice. The times are simulated.
256 devices in a mesh: img: 32 (over z, x), txt: 8 (over y, core).
Axes of the slice: x: 4, y: 4, z: 8, core: 2. Of those that a mesh axis runs over, the one named last changes fastest.
Arguments:
- image_pooled: bfloat16 [16384, 1664], P('img', 'txt'), may hold values from -6 to 6
- text_pooled: bfloat16 [16384, 1280], P('txt', 'img'), may hold values from -6 to 6
- image_proj: bfloat16 [1664, 1280], P('txt'), may hold values from -1.5 to 1.5
- text_proj: bfloat16 [1280, 1280], P('img'), may hold values from -2 to 2
- teacher_scale: float32 [1], replicated, may hold values from 280 to 400
Outputs:
- image_targets: float32 [16384, 16384], P('img', 'txt')
- text_targets: float32 [16384, 16384], P('img', 'txt')
All inputs are finite; a program needn't handle non-finite values.
Results may differ from a plain program's by a relative error of at most 0.0011.
Values may be sent and summed in bfloat16 or wider, within the bound.
No kernel may reach another device: no remote copies, remote signals or barrier semaphores. Data moves between devices by JAX's collectives and lax.ppermute only.
A program may use at most 64 MiB of HBM per device.

v0:
```python
import math

import jax
import jax.numpy as jnp
from jax import lax
from jax.sharding import PartitionSpec as P


def unit_rows(values):
    scale_rows = lax.rsqrt(jnp.mean(values * values, axis=-1, keepdims=True) + 1e-06)
    return (values * scale_rows / math.sqrt(values.shape[-1])).astype(jnp.bfloat16)


def add_rows(left_side, portion):
    return jnp.dot(left_side, portion, preferred_element_type=jnp.float32)


def on_device(image_pooled, text_pooled, image_proj, text_proj, teacher_scale):
    image_full = lax.all_gather(image_pooled, "txt", axis=1, tiled=True)
    image_sum = add_rows(image_full, lax.all_gather(image_proj, "txt", axis=0, tiled=True))
    image_unit = unit_rows(image_sum)
    weight_full = lax.all_gather(text_proj, "img", axis=0, tiled=True)
    text_full = lax.all_gather(text_pooled, "img", axis=1, tiled=True)
    text_unit = unit_rows(jnp.dot(text_full, weight_full, preferred_element_type=jnp.float32))
    similar = lax.dot_general(
        image_unit, text_unit, (((1,), (1,)), ((), ())), preferred_element_type=jnp.float32
    )
    logits = teacher_scale[0] * similar
    row_top = jnp.max(logits, axis=1, keepdims=True)
    col_top = jnp.max(logits, axis=0, keepdims=True)
    row_top = lax.pmax(row_top, "txt")
    col_top = lax.pmax(col_top, "img")
    row_total = lax.psum(jnp.sum(jnp.exp(logits - row_top), axis=1, keepdims=True), "txt")
    col_total = lax.psum(jnp.sum(jnp.exp(logits - col_top), axis=0, keepdims=True), "img")
    image_targets = logits - (row_top + jnp.log(row_total))
    text_targets = logits - (col_top + jnp.log(col_total))
    return (image_targets, text_targets)


def solution(mesh):
    placed = (P("img", "txt"), P("txt", "img"), P("txt", None), P("img", None), P())
    return jax.shard_map(
        on_device,
        mesh=mesh,
        in_specs=placed,
        out_specs=(P("img", "txt"), P("img", "txt")),
        check_vma=False,
    )
```

profile of v0, /device:TPU:32, one launch (start us, length us, event | category | flops | bytes accessed | tf_op | source)
XLA Modules:
  0.0 437.3 jit_solution(12399462446347487872)
XLA Ops:
  7.2 0.0 all-gather.5.cloned.1.call-start
  7.2 0.7 all-gather.5.cloned.1.call-update
  7.9 0.0 all-gather.7.cloned.1.call-start
  7.9 0.7 all-gather.7.cloned.1.call-update
  8.6 0.0 all-gather.11.cloned.1.call-start
  8.7 0.7 all-gather.11.cloned.1.call-update
  9.4 0.0 all-gather.9.cloned.1.call-start
  9.4 0.5 all-gather.9.cloned.1.call-update
  10.6 29.0 %all-gather.5.cloned.1.call-done = bf16[512,1664]{0,1:T(8,128)(2,1)} async-done(((bf16[512,208]{0,1:T(8,128)(2,1)}), bf16[512,1664]{0,1:T(8,128)(2,1)}) %all-gather.5.cloned.1.call-update) | async-done | bytes 1703952 | tf_op jit(solution)/shard_map/all_gather | solution.py:19
  39.6 37.1 %all-gather.7.cloned.1.call-done = bf16[1664,1280]{1,0:T(8,128)(2,1)} async-done(((bf16[208,1280]{1,0:T(8,128)(2,1)}), bf16[1664,1280]{1,0:T(8,128)(2,1)}) %all-gather.7.cloned.1.call-update) | async-done | bytes 4259856 | tf_op jit(solution)/shard_map/all_gather | solution.py:20
  76.7 5.5 %multiply_reduce_fusion.1 = (f32[512]{0:T(512)S(1)}, f32[512,1280]{1,0:T(8,128)S(1)}) fusion(bf16[512,1664]{0,1:T(8,128)(2,1)} %all-gather.5.cloned.1.call-done, bf16[1664,1280]{1,0:T(8,128)(2,1)} %all-gather.7.cloned.1.call-done), kind=kOutput, calls=%fused_computation.9 | convolution fusion | flops 2182348288 | bytes 8587264 | tf_op jit(solution)/shard_map/dot_general | solution.py:15
  82.1 76.6 %all-gather.11.cloned.1.call-done = bf16[1280,1280]{1,0:T(8,128)(2,1)} async-done(((bf16[40,1280]{1,0:T(8,128)(2,1)}), bf16[1280,1280]{1,0:T(8,128)(2,1)}) %all-gather.11.cloned.1.call-update) | async-done | bytes 3276816 | tf_op jit(solution)/shard_map/all_gather | solution.py:22
  158.7 84.9 %all-gather.9.cloned.1.call-done = bf16[2048,1280]{0,1:T(8,128)(2,1)} async-done(((bf16[2048,40]{0,1:T(8,128)(2,1)}), bf16[2048,1280]{0,1:T(8,128)(2,1)}) %all-gather.9.cloned.1.call-update) | async-done | bytes 5242896 | tf_op jit(solution)/shard_map/all_gather | solution.py:23
  243.6 10.4 %multiply_reduce_fusion = (f32[2048]{0:T(1024)S(1)}, f32[2048,1280]{0,1:T(8,128)S(1)}) fusion(bf16[2048,1280]{0,1:T(8,128)(2,1)} %all-gather.9.cloned.1.call-done, bf16[1280,1280]{1,0:T(8,128)(2,1)} %all-gather.11.cloned.1.call-done), kind=kOutput, calls=%fused_computation.1 | convolution fusion | flops 6716127232 | bytes 19013632 | tf_op jit(solution)/shard_map/dot_general | solution.py:24
  254.0 4.7 %fusion.7 = (f32[2048]{0:T(1024)S(1)}, f32[512]{0:T(512)S(1)}, f32[512,2048]{1,0:T(8,128)}) fusion(f32[2048,1280]{0,1:T(8,128)S(1)} %get-tuple-element.9, f32[2048]{0:T(1024)S(1)} %add_rsqrt_fusion, f32[512,1280]{1,0:T(8,128)S(1)} %get-tuple-element.11, f32[512]{0:T(512)S(1)} %add_rsqrt_fusion.1, f32[]{:T(128)} %bitcast.13), kind=kOutput, calls=%fused_computation.19 | convolution fusion | flops 2697328128 | bytes 17321988 | tf_op jit(solution)/shard_map/dot_general | solution.py:25
  258.7 67.0 %pmax.15 = f32[1,2048]{1,0:T(1,128)S(1)} all-reduce(f32[1,2048]{1,0:T(1,128)S(1)} %bitcast.20), channel_id=1, replica_groups=mesh['img'=32,'txt'=8] {'img'}, use_global_device_ids=true, to_apply=%region_7.0 | all-reduce | flops 2048 | bytes 16384 | tf_op jit(solution)/shard_map/pmax | solution.py:32
  325.7 12.4 %pmax.14 = f32[512,1]{0,1:T(1,128)S(1)} all-reduce(f32[512,1]{0,1:T(1,128)S(1)} %bitcast.21), channel_id=1, replica_groups=mesh['img'=32,'txt'=8] {'txt'}, use_global_device_ids=true, to_apply=%region_3.0 | all-reduce | flops 512 | bytes 4096 | tf_op jit(solution)/shard_map/pmax | solution.py:31
  338.1 3.4 exponential_reduce_fusion
  341.5 12.4 %psum.14 = f32[512,1]{0,1:T(1,128)S(1)} all-reduce(f32[512,1]{0,1:T(1,128)S(1)} %bitcast.18), channel_id=1, replica_groups=mesh['img'=32,'txt'=8] {'txt'}, use_global_device_ids=true, to_apply=%region_5.0 | all-reduce | flops 512 | bytes 4096 | tf_op jit(solution)/shard_map/psum | solution.py:33
  353.9 70.6 %psum.15 = f32[1,2048]{1,0:T(1,128)S(1)} all-reduce(f32[1,2048]{1,0:T(1,128)S(1)} %bitcast.16), channel_id=1, replica_groups=mesh['img'=32,'txt'=8] {'img'}, use_global_device_ids=true, to_apply=%region_9.0 | all-reduce | flops 2048 | bytes 16384 | tf_op jit(solution)/shard_map/psum | solution.py:34
  424.6 6.1 %broadcast_subtract_fusion = (f32[512,2048]{1,0:T(8,128)}, f32[512,2048]{1,0:T(8,128)}) fusion(f32[512,2048]{1,0:T(8,128)} %get-tuple-element.12, f32[2048]{0:T(1024)S(1)} %bitcast.15, f32[512]{0:T(512)S(1)} %bitcast.19), kind=kLoop, calls=%fused_computation.10 | loop fusion | flops 2097152 | bytes 12593152 | tf_op jit(solution)/shard_map/sub | solution.py:36
  (4 shorter events, 0.0 us)
Async XLA Ops:
  7.2 32.4 %all-gather.5.cloned.1.call-start = ((), (), s32[]{:S(2)}) async-start(), calls=%async_computation | async-start | bytes 1916928 | tf_op jit(solution)/shard_map/all_gather | solution.py:19
  7.9 68.8 %all-gather.7.cloned.1.call-start = ((), (), s32[]{:S(2)}) async-start(), calls=%async_computation.1 | async-start | bytes 4792320 | tf_op jit(solution)/shard_map/all_gather | solution.py:20
  8.6 150.1 %all-gather.11.cloned.1.call-start = ((), (), s32[]{:S(2)}) async-start(), calls=%async_computation.3 | async-start | bytes 3379200 | tf_op jit(solution)/shard_map/all_gather | solution.py:22
  9.4 234.2 %all-gather.9.cloned.1.call-start = ((), (), s32[]{:S(2)}) async-start(), calls=%async_computation.2 | async-start | bytes 5406720 | tf_op jit(solution)/shard_map/all_gather | solution.py:23
Sparse Core Ops, SparseCore 0:
  9.8 29.7 all-gather.4
  41.4 35.2 all-gather.6
  79.3 79.4 all-gather.10
  161.2 82.3 all-gather.8
where the time goes:
time: 445 us; the launch traced here: 437 us
  waiting for transfers between devices  230 us (52%)
  blocking collectives  162 us (36%)
  matrix products  20.6 us (5%)
  between operations  14.4 us (3%)
  other arithmetic  9.6 us (2%)
    all_gather x1, waiting for transfers between devices, on_device(): text_full = lax.all_gather(text_pooled, 'img', axis=1, tiled=True)  84.9 us
    all_gather x1, waiting for transfers between devices, on_device(): weight_full = lax.all_gather(text_proj, 'img', axis=0, tiled=True)  76.6 us
    psum x1, blocking collectives, on_device(): lax.psum(jnp.sum(jnp.exp(logits - col_top), axis=0, keepdims=True), 'img')  70.6 us
    pmax x1, blocking collectives, on_device(): col_top = lax.pmax(col_top, 'img')  67 us
    all_gather x1, waiting for transfers between devices, on_device(): lax.all_gather(image_proj, 'txt', axis=0, tiled=True)  37.1 us
    all_gather x1, waiting for transfers between devices, on_device(): image_full = lax.all_gather(image_pooled, 'txt', axis=1, tiled=True)  29 us
    pmax x1, blocking collectives, on_device(): row_top = lax.pmax(row_top, 'txt')  12.4 us
    psum x1, blocking collectives, on_device(): lax.psum(jnp.sum(jnp.exp(logits - row_top), axis=1, keepdims=True), 'txt')  12.4 us
  transfers between devices with their start and end apart: 4, of which 4 were waited for; matrix products, arithmetic and copies ran while one was open for 1% of the time, Pallas kernels for 0%

commit v1 on v0

v1 whole, which is shorter than its diff:
```python
import math

import jax
import jax.numpy as jnp
from jax import lax
from jax.sharding import Mesh, PartitionSpec as P

SIZES = {"z": 8, "x": 4, "y": 4, "core": 2}
IMG = ("z", "x")
TXT = ("y", "core")
ROWS_A = 768


def shift(value, axis, step):
    count = SIZES[axis]
    return lax.ppermute(value, axis, [(i, (i + step) % count) for i in range(count)])


def unit_rows(values):
    scale_rows = lax.rsqrt(jnp.mean(values * values, axis=-1, keepdims=True) + 1e-06)
    return (values * scale_rows / math.sqrt(values.shape[-1])).astype(jnp.bfloat16)


def along_x(block):
    return [block, shift(block, "x", 1), shift(block, "x", -1), shift(block, "x", 2)]


def along_x_forwarding(block):
    half = block.shape[0] // 2
    ahead, back = shift(block, "x", 1), shift(block, "x", -1)
    far = [shift(ahead[:half], "x", 1), shift(back[half:], "x", -1)]
    return [block, ahead, back, jnp.concatenate(far, axis=0)]


def along_z(block, cut):
    ahead, back = [block], [block]
    for _ in range(3):
        ahead.append(shift(ahead[-1], "z", 1))
        back.append(shift(back[-1], "z", -1))
    half = block.shape[cut] // 2
    first = lax.slice_in_dim(ahead[3], 0, half, axis=cut)
    second = lax.slice_in_dim(back[3], half, 2 * half, axis=cut)
    far = jnp.concatenate([shift(first, "z", 1), shift(second, "z", -1)], axis=cut)
    return ahead + [far] + back[:0:-1]


def lse_over(local, axes, count):
    spread = jnp.broadcast_to(local[None], (count,) + local.shape)
    parts = lax.all_to_all(spread, axes, 0, 0)
    top = jnp.max(parts, axis=0)
    return top + jnp.log(jnp.sum(jnp.exp(parts - top), axis=0))


def on_device(image_pooled, text_pooled, image_proj, text_proj, teacher_scale):
    core = lax.axis_index("core")
    width = text_proj.shape[1] // 2
    text_lines = text_pooled.T
    own = lax.dynamic_slice_in_dim(text_proj, core * width, width, axis=1)
    block_a = jnp.concatenate([text_lines[:, :ROWS_A], own], axis=1)
    block_b = text_lines[:, ROWS_A:]

    partial = jnp.dot(image_pooled, image_proj, preferred_element_type=jnp.float32)
    image_part = lax.psum_scatter(partial, TXT, scatter_dimension=0, tiled=True)
    image_unit = lax.all_gather(unit_rows(image_part), TXT, axis=0, tiled=True)

    full_a = jnp.concatenate(along_z(jnp.concatenate(along_x(block_a), axis=0), 0), axis=0)
    full_b = jnp.concatenate(along_x_forwarding(jnp.concatenate(along_z(block_b, 1), axis=0)), axis=0)
    depth, rest = text_lines.shape[0], block_b.shape[1]
    full_b = full_b.reshape(4, 8, depth, rest).transpose(1, 0, 2, 3).reshape(32 * depth, rest)
    weight_own = full_a[:, ROWS_A:]
    weight = jnp.concatenate([weight_own, shift(weight_own, "core", 1)], axis=1)
    text_full = jnp.concatenate([full_a[:, :ROWS_A], full_b], axis=1)
    text_sum = lax.dot_general(
        text_full, weight, (((0,), (0,)), ((), ())), preferred_element_type=jnp.float32
    )
    text_unit = unit_rows(text_sum)
    image_unit = jnp.where(core == 0, image_unit, jnp.roll(image_unit, width, axis=1))
    similar = lax.dot_general(
        image_unit, text_unit, (((1,), (1,)), ((), ())), preferred_element_type=jnp.float32
    )
    logits = teacher_scale[0] * similar
    row_top = jnp.max(logits, axis=1)
    col_top = jnp.max(logits, axis=0)
    row_part = row_top + jnp.log(jnp.sum(jnp.exp(logits - row_top[:, None]), axis=1))
    col_part = col_top + jnp.log(jnp.sum(jnp.exp(logits - col_top[None, :]), axis=0))
    row_lse = lse_over(row_part.reshape(4, 128), TXT, 8).reshape(-1)
    col_lse = lse_over(col_part.reshape(16, 128), IMG, 32).reshape(-1)
    return (logits - row_lse[:, None], logits - col_lse[None, :])


def solution(mesh):
    grid = Mesh(mesh.devices.reshape(8, 4, 4, 2), ("z", "x", "y", "core"))
    placed = (P(IMG, TXT), P(TXT, IMG), P(TXT, None), P(IMG, None), P())
    return jax.shard_map(
        on_device,
        mesh=grid,
        in_specs=placed,
        out_specs=(P(IMG, TXT), P(IMG, TXT)),
        check_vma=False,
    )
```

time: 445 us -> 176 us (0.40); the launches traced: 437 us -> 175 us
  waiting for transfers between devices: 230 us -> 47.5 us
  blocking collectives: 162 us -> 0 us
  starting transfers between devices: 0.15 us -> 50.3 us
  local copies, waits for them, and re-layouts: 0 us -> 29.8 us
    all_gather x4 -> x1, waiting for transfers between devices: 227 us -> 7.98 us  [on_device(): image_unit = lax.all_gather(unit_rows(image_part), TXT, axis=0, tiled=True)]
    psum x2 -> x0, blocking collectives: 83.1 us -> none  [the longest x1 70.6 us: on_device(): lax.psum(jnp.sum(jnp.exp(logits - col_top), axis=0, keepdims=True), 'img')]
    pmax x2 -> x0, blocking collectives: 79.4 us -> none  [the longest x1 67 us: on_device(): col_top = lax.pmax(col_top, 'img')]
    ppermute x0 -> x24, starting transfers between devices: none -> 36.8 us  [shift(): lax.ppermute(value, axis, [(i, (i + step) % count) for i in range(count)])]
    ppermute x0 -> x24, waiting for transfers between devices: none -> 22.1 us  [shift(): lax.ppermute(value, axis, [(i, (i + step) % count) for i in range(count)])]
    unnamed x0 -> x31, local copies, waits for them, and re-layouts: none -> 18.4 us
    all_to_all x0 -> x2, waiting for transfers between devices: none -> 17.3 us  [lse_over(): parts = lax.all_to_all(spread, axes, 0, 0)]
    all_to_all x0 -> x2, starting transfers between devices: none -> 13.4 us  [lse_over(): parts = lax.all_to_all(spread, axes, 0, 0)]
  transfers between devices with their start and end apart: 4 -> 28, of which waited for: 4 -> 13; matrix products, arithmetic and copies ran while one was open for 1% -> 23% of each run, Pallas kernels for 0% -> 0%
where the time goes in v1:
time: 176 us; the launch traced here: 175 us
  starting transfers between devices  50.3 us (29%)
  waiting for transfers between devices  47.5 us (27%)
  local copies, waits for them, and re-layouts  29.8 us (17%)
  matrix products  21 us (12%)
  between operations  14.9 us (8%)
  other arithmetic  11.8 us (7%)
    ppermute x24, starting transfers between devices, shift(): lax.ppermute(value, axis, [(i, (i + step) % count) for i in range(count)])  36.8 us
    ppermute x24, waiting for transfers between devices, shift(): lax.ppermute(value, axis, [(i, (i + step) % count) for i in range(count)])  22.1 us
    unnamed x31, local copies, waits for them, and re-layouts  18.4 us
    all_to_all x2, waiting for transfers between devices, lse_over(): parts = lax.all_to_all(spread, axes, 0, 0)  17.3 us
    all_to_all x2, starting transfers between devices, lse_over(): parts = lax.all_to_all(spread, axes, 0, 0)  13.4 us
    dot_general x1, matrix products, on_device(): lax.dot_general(text_full, weight, (((0,), (0,)), ((), ())), preferred_el...  11.8 us
    all_gather x1, waiting for transfers between devices, on_device(): image_unit = lax.all_gather(unit_rows(image_part), TXT, axis=0, tiled=True)  7.98 us
    dot_general x1, matrix products, on_device(): lax.dot_general(image_unit, text_unit, (((1,), (1,)), ((), ())), preferre...  6.2 us
  transfers between devices with their start and end apart: 28, of which 13 were waited for; matrix products, arithmetic and copies ran while one was open for 23% of the time, Pallas kernels for 0%

profile of v1, /device:TPU:32, one launch (start us, length us, event | category | flops | bytes accessed | tf_op | source)
XLA Modules:
  0.0 175.3 jit_solution(10574458605559949196)
XLA Ops:
  8.2 3.0 %fusion.19 = f32[512,1280]{1,0:T(8,128)} fusion(bf16[512,208]{0,1:T(8,128)(2,1)} %param.5, bf16[208,1280]{1,0:T(8,128)(2,1)S(1)} %copy-done), kind=kOutput, calls=%fused_computation.72 | convolution fusion | flops 272629760 | bytes 3366912 | tf_op jit(solution)/shard_map/dot_general | solution.py:62
  22.4 2.1 %collective-permute-start.16 = (bf16[40,1280]{1,0:T(8,128)(2,1)S(1)}, bf16[40,1280]{1,0:T(8,128)(2,1)S(1)}, u32[]{:S(2)}, u32[]{:S(2)}) collective-permute-start(bf16[40,1280]{1,0:T(8,128)(2,1)S(1)} %collective-permute-done.15), channel_id=1, source_target_pairs={{0,224},{32,0},{64,32},{96,64},{128,96},{160,128},{192,160},{224,1... | collective-permute-start | bytes 307208 | tf_op jit(solution)/shard_map/ppermute | solution.py:16
  26.3 2.3 %collective-permute-start.7 = (bf16[160,1408]{1,0:T(8,128)(2,1)S(1)}, bf16[160,1408]{1,0:T(8,128)(2,1)S(1)}, u32[]{:S(2)}, u32[]{:S(2)}) collective-permute-start(bf16[160,1408]{1,0:T(8,128)(2,1)S(1)} %pad_maximum_fusion), channel_id=1, source_target_pairs={{0,224},{32,0},{64,32},{96,64},{128,96},{160,128},{192,160},{224,1... | collective-permute-start | bytes 1351688 | tf_op jit(solution)/shard_map/ppermute | solution.py:16
  30.2 2.3 %collective-permute-start.17 = (bf16[40,1280]{1,0:T(8,128)(2,1)S(1)}, bf16[40,1280]{1,0:T(8,128)(2,1)S(1)}, u32[]{:S(2)}, u32[]{:S(2)}) collective-permute-start(bf16[40,1280]{1,0:T(8,128)(2,1)S(1)} %collective-permute-done.16), channel_id=1, source_target_pairs={{0,224},{32,0},{64,32},{96,64},{128,96},{160,128},{192,160},{224,1... | collective-permute-start | bytes 307208 | tf_op jit(solution)/shard_map/ppermute | solution.py:16
  33.2 6.3 %collective-permute-done.13 = bf16[40,1280]{1,0:T(8,128)(2,1)S(1)} collective-permute-done((bf16[40,1280]{1,0:T(8,128)(2,1)S(1)}, bf16[40,1280]{1,0:T(8,128)(2,1)S(1)}, u32[]{:S(2)}, u32[]{:S(2)}) %collective-permute-start.13) | collective-permute-done | bytes 102432 | tf_op jit(solution)/shard_map/ppermute | solution.py:16
  40.2 2.3 %collective-permute-start.18 = (bf16[40,640]{1,0:T(8,128)(2,1)S(1)}, bf16[40,640]{1,0:T(8,128)(2,1)S(1)}, u32[]{:S(2)}, u32[]{:S(2)}) collective-permute-start(bf16[40,640]{1,0:T(8,128)(2,1)S(1)} %slice.58), channel_id=1, source_target_pairs={{0,224},{32,0},{64,32},{96,64},{128,96},{160,128},{192,160},{224,1... | collective-permute-start | bytes 153608 | tf_op jit(solution)/shard_map/ppermute | solution.py:16
  49.2 2.9 %collective-permute-start.20 = (bf16[320,1280]{1,0:T(8,128)(2,1)}, bf16[320,1280]{1,0:T(8,128)(2,1)S(1)}, u32[]{:S(2)}, u32[]{:S(2)}) collective-permute-start(bf16[320,1280]{1,0:T(8,128)(2,1)} %get-tuple-element.15), channel_id=1, source_target_pairs={{0,24},{8,0},{16,8},{24,16},{1,25},{9,1},{17,9},{25,17},{2,26},{10... | collective-permute-start | bytes 2457608 | tf_op jit(solution)/shard_map/ppermute | solution.py:16
  52.1 3.3 %collective-permute-start.4 = (bf16[160,1408]{1,0:T(8,128)(2,1)S(1)}, bf16[160,1408]{1,0:T(8,128)(2,1)S(1)}, u32[]{:S(2)}, u32[]{:S(2)}) collective-permute-start(bf16[160,1408]{1,0:T(8,128)(2,1)S(1)} %collective-permute-done.3), channel_id=1, source_target_pairs={{0,32},{32,64},{64,96},{96,128},{128,160},{160,192},{192,224},{224... | collective-permute-start | bytes 1351688 | tf_op jit(solution)/shard_map/ppermute | solution.py:16
  56.7 6.2 %collective-permute-done.4 = bf16[160,1408]{1,0:T(8,128)(2,1)S(1)} collective-permute-done((bf16[160,1408]{1,0:T(8,128)(2,1)S(1)}, bf16[160,1408]{1,0:T(8,128)(2,1)S(1)}, u32[]{:S(2)}, u32[]{:S(2)}) %collective-permute-start.4) | collective-permute-done | bytes 450592 | tf_op jit(solution)/shard_map/ppermute | solution.py:16
  62.9 4.0 %collective-permute-start.5 = (bf16[160,1408]{1,0:T(8,128)(2,1)S(1)}, bf16[160,1408]{1,0:T(8,128)(2,1)S(1)}, u32[]{:S(2)}, u32[]{:S(2)}) collective-permute-start(bf16[160,1408]{1,0:T(8,128)(2,1)S(1)} %collective-permute-done.4), channel_id=1, source_target_pairs={{0,32},{32,64},{64,96},{96,128},{128,160},{160,192},{192,224},{224... | collective-permute-start | bytes 1351688 | tf_op jit(solution)/shard_map/ppermute | solution.py:16
  69.9 3.2 %collective-permute-start.22 = (bf16[160,1280]{1,0:T(8,128)(2,1)}, bf16[160,1280]{1,0:T(8,128)(2,1)S(1)}, u32[]{:S(2)}, u32[]{:S(2)}) collective-permute-start(bf16[160,1280]{1,0:T(8,128)(2,1)} %slice.60), channel_id=1, source_target_pairs={{0,24},{8,0},{16,8},{24,16},{1,25},{9,1},{17,9},{25,17},{2,26},{10... | collective-permute-start | bytes 1228808 | tf_op jit(solution)/shard_map/ppermute | solution.py:16
  75.2 2.6 %collective-permute-start.6 = (bf16[80,1408]{1,0:T(8,128)(2,1)S(1)}, bf16[80,1408]{1,0:T(8,128)(2,1)S(1)}, u32[]{:S(2)}, u32[]{:S(2)}) collective-permute-start(bf16[80,1408]{1,0:T(8,128)(2,1)S(1)} %slice.53), channel_id=1, source_target_pairs={{0,32},{32,64},{64,96},{96,128},{128,160},{160,192},{192,224},{224... | collective-permute-start | bytes 675848 | tf_op jit(solution)/shard_map/ppermute | solution.py:16
  79.1 2.2 %collective-permute-done.6 = bf16[80,1408]{1,0:T(8,128)(2,1)S(1)} collective-permute-done((bf16[80,1408]{1,0:T(8,128)(2,1)S(1)}, bf16[80,1408]{1,0:T(8,128)(2,1)S(1)}, u32[]{:S(2)}, u32[]{:S(2)}) %collective-permute-start.6) | collective-permute-done | bytes 225312 | tf_op jit(solution)/shard_map/ppermute | solution.py:16
  82.0 2.3 %collective-permute-done.10 = bf16[80,1408]{1,0:T(8,128)(2,1)S(1)} collective-permute-done((bf16[80,1408]{1,0:T(8,128)(2,1)S(1)}, bf16[80,1408]{1,0:T(8,128)(2,1)S(1)}, u32[]{:S(2)}, u32[]{:S(2)}) %collective-permute-start.10) | collective-permute-done | bytes 225312 | tf_op jit(solution)/shard_map/ppermute | solution.py:16
  87.4 2.7 %slice.61 = bf16[1280,640]{1,0:T(8,128)(2,1)} slice(bf16[1280,1408]{1,0:T(8,128)(2,1)} %constant_dynamic-update-slice_fusion), slice={[0:1280], [768:1408]} | slice | bytes 3276800 | tf_op jit(solution)/shard_map/slice | solution.py:70
  96.5 2.6 %copy.9 = bf16[4,8,40,1280]{3,2,0,1:T(8,128)(2,1)S(1)} copy(bf16[4,8,40,1280]{3,2,1,0:T(8,128)(2,1)} %bitcast.17) | data formatting | bytes 6553600 | tf_op jit(solution)/shard_map/reshape | solution.py:69
  99.3 11.8 %multiply_reduce_fusion = (f32[2048]{0:T(1024)S(1)}, f32[2048,1280]{0,1:T(8,128)}) fusion(bf16[1280,640]{1,0:T(8,128)(2,1)} %collective-permute-done.23, bf16[1280,640]{1,0:T(8,128)(2,1)} %slice.61, bf16[1280,1280]{1,0:T(8,128)(2,1)S(1)} %bitcast.18, bf16[1280,768]{1,0:T(8,128)(2,1)S(1)} %slice.55), kind=kOutput, calls=%fused_computation.1 | convolution fusion | flops 6733166592 | bytes 19013632 | tf_op jit(solution)/shard_map/dot_general | solution.py:73
  111.1 8.0 %all-gather.2.cloned.1.call-done = bf16[512,1280]{1,0:T(8,128)(2,1)} async-done(((bf16[64,1280]{1,0:T(8,128)(2,1)}), bf16[512,1280]{1,0:T(8,128)(2,1)}) %all-gather.2.cloned.1.call-update) | async-done | bytes 1310736 | tf_op jit(solution)/shard_map/all_gather | solution.py:64
  120.5 6.2 %fusion.17 = (f32[2048]{0:T(1024)S(1)}, f32[512]{0:T(512)S(1)}, f32[512,2048]{1,0:T(8,128)S(1)}) fusion(f32[2048,1280]{0,1:T(8,128)} %get-tuple-element.28, f32[2048]{0:T(1024)S(1)} %add_rsqrt_fusion, bf16[512,1280]{1,0:T(8,128)(2,1)} %all-gather.2.cloned.1.call-done, bf16[512,640]{1,0:T(8,128)(2,1)S(1)} %get-tuple-element.9, ...), kind=kOutput, calls=%fused_computation.70 | convolution fusion | flops 2698638848 | bytes 17319940 | tf_op jit(solution)/shard_map/dot_general | solution.py:78
  130.6 3.3 %all-to-all-start = ((f32[8,4,128]{2,1,0:T(4,128)}), f32[8,4,128]{2,1,0:T(4,128)S(1)}, u32[]{:S(2)}, u32[]{:S(2)}) async-start(f32[8,4,128]{2,1,0:T(4,128)} %broadcast_in_dim.4), calls=%async_computation.1 | async-start | bytes 32768 | tf_op jit(solution)/shard_map/all_to_all | solution.py:49
  134.0 5.3 %all-to-all-done = f32[8,4,128]{2,1,0:T(4,128)S(1)} async-done(((f32[8,4,128]{2,1,0:T(4,128)}), f32[8,4,128]{2,1,0:T(4,128)S(1)}, u32[]{:S(2)}, u32[]{:S(2)}) %all-to-all-start) | async-done | bytes 16416 | tf_op jit(solution)/shard_map/all_to_all | solution.py:49
  139.9 10.1 %all-to-all-start.1 = ((f32[32,16,128]{2,1,0:T(8,128)}), f32[32,16,128]{2,1,0:T(8,128)S(1)}, u32[]{:S(2)}, u32[]{:S(2)}) async-start(f32[32,16,128]{2,1,0:T(8,128)} %broadcast_in_dim.5), calls=%async_computation.2 | async-start | bytes 524288 | tf_op jit(solution)/shard_map/all_to_all | solution.py:49
  150.1 12.1 %all-to-all-done.1 = f32[32,16,128]{2,1,0:T(8,128)S(1)} async-done(((f32[32,16,128]{2,1,0:T(8,128)}), f32[32,16,128]{2,1,0:T(8,128)S(1)}, u32[]{:S(2)}, u32[]{:S(2)}) %all-to-all-start.1) | async-done | bytes 262176 | tf_op jit(solution)/shard_map/all_to_all | solution.py:49
  162.3 6.1 %broadcast_subtract_fusion = (f32[512,2048]{1,0:T(8,128)}, f32[512,2048]{1,0:T(8,128)}) fusion(f32[512,2048]{1,0:T(8,128)} %copy-done.1, f32[2048]{0:T(1024)S(1)} %add_bitcast_fusion, f32[512]{0:T(512)S(1)} %add_bitcast_fusion.2), kind=kLoop, calls=%fused_computation.15 | loop fusion | flops 2097152 | bytes 12593152 | tf_op jit(solution)/shard_map/sub | solution.py:88
  (102 shorter events, 47.1 us)
Async XLA Ops:
  7.2 83.0 %reduce-scatter.2.cloned.1.call-start = ((), (), s32[]{:S(2)}) async-start(), calls=%async_computation.3 | async-start | bytes 2949120 | tf_op jit(solution)/shard_map/reduce_scatter | solution.py:63
  11.2 107.8 %all-gather.2.cloned.1.call-start = ((), (), s32[]{:S(2)}) async-start(), calls=%async_computation.4 | async-start | bytes 1474560 | tf_op jit(solution)/shard_map/all_gather | solution.py:64
  12.0 8.4 %collective-permute-start.11 = (bf16[40,1280]{1,0:T(8,128)(2,1)S(1)}, bf16[40,1280]{1,0:T(8,128)(2,1)S(1)}, u32[]{:S(2)}, u32[]{:S(2)}) collective-permute-start(bf16[40,1280]{1,0:T(8,128)(2,1)S(1)} %get-tuple-element.12), channel_id=1, source_target_pairs={{0,32},{32,64},{64,96},{96,128},{128,160},{160,192},{192,224},{224... | collective-permute-start | bytes 307208 | tf_op jit(solution)/shard_map/ppermute | solution.py:16
  13.9 8.5 %collective-permute-start.15 = (bf16[40,1280]{1,0:T(8,128)(2,1)S(1)}, bf16[40,1280]{1,0:T(8,128)(2,1)S(1)}, u32[]{:S(2)}, u32[]{:S(2)}) collective-permute-start(bf16[40,1280]{1,0:T(8,128)(2,1)S(1)} %get-tuple-element.12), channel_id=1, source_target_pairs={{0,224},{32,0},{64,32},{96,64},{128,96},{160,128},{192,160},{224,1... | collective-permute-start | bytes 307208 | tf_op jit(solution)/shard_map/ppermute | solution.py:16
  14.7 10.5 %collective-permute-start = (bf16[40,1408]{1,0:T(8,128)(2,1)S(1)}, bf16[40,1408]{1,0:T(8,128)(2,1)S(1)}, u32[]{:S(2)}, u32[]{:S(2)}) collective-permute-start(bf16[40,1408]{1,0:T(8,128)(2,1)S(1)} %get-tuple-element.13), channel_id=1, source_target_pairs={{0,8},{8,16},{16,24},{24,0},{1,9},{9,17},{17,25},{25,1},{2,10},{10... | collective-permute-start | bytes 337928 | tf_op jit(solution)/shard_map/ppermute | solution.py:16
  16.2 9.0 %collective-permute-start.1 = (bf16[40,1408]{1,0:T(8,128)(2,1)S(1)}, bf16[40,1408]{1,0:T(8,128)(2,1)S(1)}, u32[]{:S(2)}, u32[]{:S(2)}) collective-permute-start(bf16[40,1408]{1,0:T(8,128)(2,1)S(1)} %get-tuple-element.13), channel_id=1, source_target_pairs={{0,24},{8,0},{16,8},{24,16},{1,25},{9,1},{17,9},{25,17},{2,26},{10... | collective-permute-start | bytes 337928 | tf_op jit(solution)/shard_map/ppermute | solution.py:16
  17.9 7.3 %collective-permute-start.2 = (bf16[40,1408]{1,0:T(8,128)(2,1)S(1)}, bf16[40,1408]{1,0:T(8,128)(2,1)S(1)}, u32[]{:S(2)}, u32[]{:S(2)}) collective-permute-start(bf16[40,1408]{1,0:T(8,128)(2,1)S(1)} %get-tuple-element.13), channel_id=1, source_target_pairs={{0,16},{8,24},{16,0},{24,8},{1,17},{9,25},{17,1},{25,9},{2,18},{10... | collective-permute-start | bytes 337928 | tf_op jit(solution)/shard_map/ppermute | solution.py:16
  20.4 8.8 %collective-permute-start.12 = (bf16[40,1280]{1,0:T(8,128)(2,1)S(1)}, bf16[40,1280]{1,0:T(8,128)(2,1)S(1)}, u32[]{:S(2)}, u32[]{:S(2)}) collective-permute-start(bf16[40,1280]{1,0:T(8,128)(2,1)S(1)} %collective-permute-done.11), channel_id=1, source_target_pairs={{0,32},{32,64},{64,96},{96,128},{128,160},{160,192},{192,224},{224... | collective-permute-start | bytes 307208 | tf_op jit(solution)/shard_map/ppermute | solution.py:16
  22.4 7.7 %collective-permute-start.16 = (bf16[40,1280]{1,0:T(8,128)(2,1)S(1)}, bf16[40,1280]{1,0:T(8,128)(2,1)S(1)}, u32[]{:S(2)}, u32[]{:S(2)}) collective-permute-start(bf16[40,1280]{1,0:T(8,128)(2,1)S(1)} %collective-permute-done.15), channel_id=1, source_target_pairs={{0,224},{32,0},{64,32},{96,64},{128,96},{160,128},{192,160},{224,1... | collective-permute-start | bytes 307208 | tf_op jit(solution)/shard_map/ppermute | solution.py:16
  25.3 26.8 %collective-permute-start.3 = (bf16[160,1408]{1,0:T(8,128)(2,1)S(1)}, bf16[160,1408]{1,0:T(8,128)(2,1)S(1)}, u32[]{:S(2)}, u32[]{:S(2)}) collective-permute-start(bf16[160,1408]{1,0:T(8,128)(2,1)S(1)} %pad_maximum_fusion), channel_id=1, source_target_pairs={{0,32},{32,64},{64,96},{96,128},{128,160},{160,192},{192,224},{224... | collective-permute-start | bytes 1351688 | tf_op jit(solution)/shard_map/ppermute | solution.py:16
  26.3 29.1 %collective-permute-start.7 = (bf16[160,1408]{1,0:T(8,128)(2,1)S(1)}, bf16[160,1408]{1,0:T(8,128)(2,1)S(1)}, u32[]{:S(2)}, u32[]{:S(2)}) collective-permute-start(bf16[160,1408]{1,0:T(8,128)(2,1)S(1)} %pad_maximum_fusion), channel_id=1, source_target_pairs={{0,224},{32,0},{64,32},{96,64},{128,96},{160,128},{192,160},{224,1... | collective-permute-start | bytes 1351688 | tf_op jit(solution)/shard_map/ppermute | solution.py:16
  29.2 10.2 %collective-permute-start.13 = (bf16[40,1280]{1,0:T(8,128)(2,1)S(1)}, bf16[40,1280]{1,0:T(8,128)(2,1)S(1)}, u32[]{:S(2)}, u32[]{:S(2)}) collective-permute-start(bf16[40,1280]{1,0:T(8,128)(2,1)S(1)} %collective-permute-done.12), channel_id=1, source_target_pairs={{0,32},{32,64},{64,96},{96,128},{128,160},{160,192},{192,224},{224... | collective-permute-start | bytes 307208 | tf_op jit(solution)/shard_map/ppermute | solution.py:16
  30.2 10.0 %collective-permute-start.17 = (bf16[40,1280]{1,0:T(8,128)(2,1)S(1)}, bf16[40,1280]{1,0:T(8,128)(2,1)S(1)}, u32[]{:S(2)}, u32[]{:S(2)}) collective-permute-start(bf16[40,1280]{1,0:T(8,128)(2,1)S(1)} %collective-permute-done.16), channel_id=1, source_target_pairs={{0,224},{32,0},{64,32},{96,64},{128,96},{160,128},{192,160},{224,1... | collective-permute-start | bytes 307208 | tf_op jit(solution)/shard_map/ppermute | solution.py:16
  48.8 20.1 %collective-permute-start.19 = (bf16[320,1280]{1,0:T(8,128)(2,1)}, bf16[320,1280]{1,0:T(8,128)(2,1)S(1)}, u32[]{:S(2)}, u32[]{:S(2)}) collective-permute-start(bf16[320,1280]{1,0:T(8,128)(2,1)} %get-tuple-element.15), channel_id=1, source_target_pairs={{0,8},{8,16},{16,24},{24,0},{1,9},{9,17},{17,25},{25,1},{2,10},{10... | collective-permute-start | bytes 2457608 | tf_op jit(solution)/shard_map/ppermute | solution.py:16
  49.2 19.9 %collective-permute-start.20 = (bf16[320,1280]{1,0:T(8,128)(2,1)}, bf16[320,1280]{1,0:T(8,128)(2,1)S(1)}, u32[]{:S(2)}, u32[]{:S(2)}) collective-permute-start(bf16[320,1280]{1,0:T(8,128)(2,1)} %get-tuple-element.15), channel_id=1, source_target_pairs={{0,24},{8,0},{16,8},{24,16},{1,25},{9,1},{17,9},{25,17},{2,26},{10... | collective-permute-start | bytes 2457608 | tf_op jit(solution)/shard_map/ppermute | solution.py:16
  52.1 10.8 %collective-permute-start.4 = (bf16[160,1408]{1,0:T(8,128)(2,1)S(1)}, bf16[160,1408]{1,0:T(8,128)(2,1)S(1)}, u32[]{:S(2)}, u32[]{:S(2)}) collective-permute-start(bf16[160,1408]{1,0:T(8,128)(2,1)S(1)} %collective-permute-done.3), channel_id=1, source_target_pairs={{0,32},{32,64},{64,96},{96,128},{128,160},{160,192},{192,224},{224... | collective-permute-start | bytes 1351688 | tf_op jit(solution)/shard_map/ppermute | solution.py:16
  55.4 11.9 %collective-permute-start.8 = (bf16[160,1408]{1,0:T(8,128)(2,1)S(1)}, bf16[160,1408]{1,0:T(8,128)(2,1)S(1)}, u32[]{:S(2)}, u32[]{:S(2)}) collective-permute-start(bf16[160,1408]{1,0:T(8,128)(2,1)S(1)} %collective-permute-done.7), channel_id=1, source_target_pairs={{0,224},{32,0},{64,32},{96,64},{128,96},{160,128},{192,160},{224,1... | collective-permute-start | bytes 1351688 | tf_op jit(solution)/shard_map/ppermute | solution.py:16
  62.9 12.3 %collective-permute-start.5 = (bf16[160,1408]{1,0:T(8,128)(2,1)S(1)}, bf16[160,1408]{1,0:T(8,128)(2,1)S(1)}, u32[]{:S(2)}, u32[]{:S(2)}) collective-permute-start(bf16[160,1408]{1,0:T(8,128)(2,1)S(1)} %collective-permute-done.4), channel_id=1, source_target_pairs={{0,32},{32,64},{64,96},{96,128},{128,160},{160,192},{192,224},{224... | collective-permute-start | bytes 1351688 | tf_op jit(solution)/shard_map/ppermute | solution.py:16
  67.3 10.8 %collective-permute-start.9 = (bf16[160,1408]{1,0:T(8,128)(2,1)S(1)}, bf16[160,1408]{1,0:T(8,128)(2,1)S(1)}, u32[]{:S(2)}, u32[]{:S(2)}) collective-permute-start(bf16[160,1408]{1,0:T(8,128)(2,1)S(1)} %collective-permute-done.8), channel_id=1, source_target_pairs={{0,224},{32,0},{64,32},{96,64},{128,96},{160,128},{192,160},{224,1... | collective-permute-start | bytes 1351688 | tf_op jit(solution)/shard_map/ppermute | solution.py:16
  69.0 25.9 %collective-permute-start.21 = (bf16[160,1280]{1,0:T(8,128)(2,1)S(1)}, bf16[160,1280]{1,0:T(8,128)(2,1)S(1)}, u32[]{:S(2)}, u32[]{:S(2)}) collective-permute-start(bf16[160,1280]{1,0:T(8,128)(2,1)S(1)} %slice.59), channel_id=1, source_target_pairs={{0,8},{8,16},{16,24},{24,0},{1,9},{9,17},{17,25},{25,1},{2,10},{10... | collective-permute-start | bytes 1228808 | tf_op jit(solution)/shard_map/ppermute | solution.py:16
  69.9 25.8 %collective-permute-start.22 = (bf16[160,1280]{1,0:T(8,128)(2,1)}, bf16[160,1280]{1,0:T(8,128)(2,1)S(1)}, u32[]{:S(2)}, u32[]{:S(2)}) collective-permute-start(bf16[160,1280]{1,0:T(8,128)(2,1)} %slice.60), channel_id=1, source_target_pairs={{0,24},{8,0},{16,8},{24,16},{1,25},{9,1},{17,9},{25,17},{2,26},{10... | collective-permute-start | bytes 1228808 | tf_op jit(solution)/shard_map/ppermute | solution.py:16
  90.1 9.1 %collective-permute-start.23 = (bf16[1280,640]{1,0:T(8,128)(2,1)}, bf16[1280,640]{1,0:T(8,128)(2,1)}, u32[]{:S(2)}, u32[]{:S(2)}) collective-permute-start(bf16[1280,640]{1,0:T(8,128)(2,1)} %slice.61), channel_id=1, source_target_pairs={{0,1},{1,0},{2,3},{3,2},{4,5},{5,4},{6,7},{7,6},{8,9},{9,8},{10,11... | collective-permute-start | bytes 4915208 | tf_op jit(solution)/shard_map/ppermute | solution.py:16
  130.6 8.6 %all-to-all-start = ((f32[8,4,128]{2,1,0:T(4,128)}), f32[8,4,128]{2,1,0:T(4,128)S(1)}, u32[]{:S(2)}, u32[]{:S(2)}) async-start(f32[8,4,128]{2,1,0:T(4,128)} %broadcast_in_dim.4), calls=%async_computation.1 | async-start | bytes 32768 | tf_op jit(solution)/shard_map/all_to_all | solution.py:49
  139.9 22.2 %all-to-all-start.1 = ((f32[32,16,128]{2,1,0:T(8,128)}), f32[32,16,128]{2,1,0:T(8,128)S(1)}, u32[]{:S(2)}, u32[]{:S(2)}) async-start(f32[32,16,128]{2,1,0:T(8,128)} %broadcast_in_dim.5), calls=%async_computation.2 | async-start | bytes 524288 | tf_op jit(solution)/shard_map/all_to_all | solution.py:49
  (9 other events, 39.9 us)
Sparse Core Ops, SparseCore 0:
  11.3 39.9 reduce-scatter.1
  93.1 25.8 all-gather.1
